TPU v7x, 32 devices: a whole 2x2x4 slice. The times are simulated.
32 devices in a mesh: groups: 2 (over y), frames: 4 (over z), heads: 2 (over x), rep: 2 (over core).
Axes of the slice: x: 2, y: 2, z: 4, core: 2. Of those that a mesh axis runs over, the one named last changes fastest.
Arguments:
- query: bfloat16 [4096, 3072], P(('groups', 'frames', 'rep'), 'heads'), parts along dimension 0, may hold values from -120 to 120
- key_proj: bfloat16 [4096, 3072], P(('groups', 'frames', 'rep'), 'heads'), parts along dimension 0, may hold values from -4 to 4
- value: bfloat16 [4096, 3072], P(('groups', 'frames', 'rep'), 'heads'), parts along dimension 0, may hold values from -6 to 6
- block_mask: int32 [24, 8, 8], P('heads'), may hold values from 0 to 1, as said below
- tile_sizes: int32 [2, 4], P('rep'), may hold values from 1 to 128, 256 in all within a row
- temporal_ids: int32 [8], P('heads'), may hold values from 0 to 23, as said below
Outputs:
- attended: bfloat16 [4096, 3072], P(('groups', 'frames', 'rep'), 'heads'), parts along dimension 0
There are 2 independent parts, one for each index of `groups`. A program takes and returns all parts, laid end to end along the dimension named above; an argument that names none is the same for every part. Nothing has to cross between parts.
Inputs may be any that keep to these rules, and one draw needn't show every extreme that they name: `block_mask`: each row of each head's block mask has exactly 4 ones, its diagonal entry among them. Entries j of temporal_ids are distinct and lie in heads (j // 4) * 12 to (j // 4 + 1) * 12 - 1. `tile_sizes`: each row sums to 256, and its largest entry is 128.
All inputs are finite; a program needn't handle non-finite values.
Results may differ from a plain program's by a relative error of at most 0.008.
Values may be sent and summed in bfloat16 or wider, within the bound.
A program may use at most 64 MiB of HBM per device.

v0:
```python
import jax
import jax.numpy as jnp
from jax import lax
from jax.sharding import PartitionSpec as P

HD = 128
BLK = 64


MASKED_SCORE = -1e30


def softmax_weights(scores):
    highest = jnp.max(scores, axis=-1, keepdims=True)
    raised = jnp.exp(scores - highest)
    return (raised / jnp.sum(raised, axis=-1, keepdims=True)).astype(jnp.bfloat16)


def select_heads(token_rows, picker):
    head_grid = token_rows.reshape(token_rows.shape[0], -1, HD)
    chosen = jnp.einsum(
        "rhd,th->rtd", head_grid, picker.astype(jnp.bfloat16), preferred_element_type=jnp.float32
    )
    return chosen.astype(jnp.bfloat16)


def spread_heads(head_grid, picker):
    return jnp.einsum(
        "rtd,th->rhd", head_grid, picker.astype(jnp.bfloat16), preferred_element_type=jnp.float32
    )


def local(query, key_proj, value, block_mask, tile_sizes, temporal_ids):
    half_rows = query.shape[0]
    heads_here = block_mask.shape[0]
    temp_here = temporal_ids.shape[0]
    spat_here = heads_here - temp_here
    frame_blocks = block_mask.shape[1]
    frame_count = lax.axis_size("frames")
    slot_count = 2 * half_rows // frame_count
    score_scale = HD ** (-0.5)
    local_ids = temporal_ids - lax.axis_index("heads") * heads_here
    head_range = jnp.arange(heads_here, dtype=jnp.int32)
    pick_temp = local_ids[:, None] == head_range[None, :]
    temp_flag = jnp.sum(pick_temp.astype(jnp.int32), axis=0)
    spat_rank = jnp.cumsum(1 - temp_flag) - 1
    pick_spat = (spat_rank[None, :] == jnp.arange(spat_here, dtype=jnp.int32)[:, None]) & (
        temp_flag[None, :] == 0
    )
    tile_len = tile_sizes[0]
    starts = jnp.cumsum(tile_len) - tile_len
    slot_index = jnp.arange(slot_count, dtype=jnp.int32)
    source_rows = jnp.minimum(starts[:, None] + slot_index[None, :], half_rows - 1)
    frame_range = jnp.arange(frame_count, dtype=jnp.int32)
    own_len = jnp.sum(jnp.where(frame_range == lax.axis_index("frames"), tile_len, 0))
    key_live = jnp.tile(slot_index < own_len, frame_count)
    send_query = select_heads(query, pick_temp)[source_rows]
    send_keys = select_heads(key_proj, pick_temp)[source_rows]
    send_values = select_heads(value, pick_temp)[source_rows]
    tile_query = lax.all_to_all(send_query, "frames", split_axis=0, concat_axis=0, tiled=True)
    tile_keys = lax.all_to_all(send_keys, "frames", split_axis=0, concat_axis=0, tiled=True)
    tile_values = lax.all_to_all(send_values, "frames", split_axis=0, concat_axis=0, tiled=True)
    item_count = tile_query.shape[2]
    flat_query = tile_query.reshape(frame_count * slot_count, item_count, HD)
    flat_keys = tile_keys.reshape(frame_count * slot_count, item_count, HD)
    flat_values = tile_values.reshape(frame_count * slot_count, item_count, HD)
    scores = (
        jnp.einsum("qhd,khd->hqk", flat_query, flat_keys, preferred_element_type=jnp.float32)
        * score_scale
    )
    scores = jnp.where(key_live[None, None, :], scores, MASKED_SCORE)
    weights = softmax_weights(scores)
    tile_out = jnp.einsum(
        "hqk,khd->qhd", weights, flat_values, preferred_element_type=jnp.float32
    ).astype(jnp.bfloat16)
    returned = lax.all_to_all(
        tile_out.reshape(frame_count, slot_count, item_count, HD),
        "frames",
        split_axis=0,
        concat_axis=0,
        tiled=True,
    )
    own_keys = select_heads(key_proj, pick_spat)
    own_values = select_heads(value, pick_spat)
    spat_keys, spat_values = (
        lax.all_gather(own_keys, "rep", axis=0, tiled=True),
        lax.all_gather(own_values, "rep", axis=0, tiled=True),
    )
    spat_query = select_heads(query, pick_spat)
    spat_mask = (
        jnp.einsum("hij,th->tij", block_mask.astype(jnp.float32), pick_spat.astype(jnp.float32))
        > 0.5
    )
    query_blocks = half_rows // BLK
    mask_rows = lax.dynamic_slice_in_dim(
        spat_mask, lax.axis_index("rep") * query_blocks, query_blocks, 1
    )
    scores = (
        jnp.einsum("qhd,khd->hqk", spat_query, spat_keys, preferred_element_type=jnp.float32)
        * score_scale
    )
    shaped = scores.reshape(spat_here, query_blocks, BLK, frame_blocks, BLK)
    shaped = jnp.where(mask_rows[:, :, None, :, None], shaped, MASKED_SCORE)
    weights = softmax_weights(shaped.reshape(spat_here, half_rows, frame_blocks * BLK))
    spat_out = jnp.einsum(
        "hqk,khd->qhd", weights, spat_values, preferred_element_type=jnp.float32
    ).astype(jnp.bfloat16)
    positions = jnp.arange(half_rows, dtype=jnp.int32)
    tile_ends = starts + tile_len
    tile_of = jnp.sum((positions[:, None] >= tile_ends[None, :]).astype(jnp.int32), axis=1)
    picked_start = jnp.sum(
        jnp.where(tile_of[:, None] == frame_range[None, :], starts[None, :], 0), axis=1
    )
    flat_index = tile_of * slot_count + positions - picked_start
    temp_out = returned.reshape(frame_count * slot_count, temp_here, HD)[flat_index]
    combined = spread_heads(spat_out, pick_spat) + spread_heads(temp_out, pick_temp)
    return combined.astype(jnp.bfloat16).reshape(half_rows, heads_here * HD)


def solution(mesh):
    in_specs = (
        P(("groups", "frames", "rep"), "heads"),
        P(("groups", "frames", "rep"), "heads"),
        P(("groups", "frames", "rep"), "heads"),
        P("heads", None, None),
        P("rep", None),
        P("heads"),
    )
    out_specs = P(("groups", "frames", "rep"), "heads")
    return jax.shard_map(local, mesh=mesh, in_specs=in_specs, out_specs=out_specs, check_vma=False)
```

profile of v0, /device:TPU:0, one launch (start us, length us, event | category | flops | bytes accessed | tf_op | source)
XLA Modules:
  0.0 106.1 jit_solution(6965234729748970537)
XLA Ops:
  6.5 0.7 broadcast_subtract_fusion
  7.2 0.1 convert_reduce_fusion.1
  7.3 0.2 reduce-window.13
  7.5 1.4 %copy.75 = bf16[256,1536]{0,1:T(8,128)(2,1)S(1)} copy(bf16[256,1536]{1,0:T(8,128)(2,1)} %param.7) | data formatting | bytes 1572864 | tf_op args[1]
  8.9 1.0 copy.76
  9.9 1.1 %fusion.18 = bf16[256,8,128]{2,1,0:T(8,128)(2,1)} fusion(bf16[256,12,128]{2,1,0:T(8,128)(2,1)S(1)} %copy.76, s32[12]{0:T(128)S(1)} %add_bitcast_fusion, pred[12]{0:T(512)(128)(4,1)S(1)} %broadcast_compare_fusion), kind=kOutput, calls=%fused_computation.32 | convolution fusion | flops 6553792 | bytes 1310780 | tf_op jit(solution)/shard_map/rhd,th->rtd/dot_general | solution.py:21
  11.0 1.4 %copy.73 = bf16[256,1536]{0,1:T(8,128)(2,1)S(1)} copy(bf16[256,1536]{1,0:T(8,128)(2,1)} %param.6) | data formatting | bytes 1572864 | tf_op args[0]
  12.5 1.0 copy.74
  13.5 0.2 reduce-window.14
  13.7 0.7 bitcast_subtract_fusion.1
  14.5 0.4 fusion.20
  14.8 2.5 %gather_fusion.1 = bf16[512,4,128]{2,1,0:T(4,128)(2,1)} fusion(bf16[256,4,128]{2,1,0:T(4,128)(2,1)S(1)} %fusion.20, s32[1024]{0:T(1024)S(1)} %pad_clamp_fusion.1), kind=kCustom, calls=%fused_computation.1 | custom fusion | bytes 1050624 | tf_op jit(solution)/shard_map/gather | solution.py:57
  17.4 6.3 %all-to-all-start.1 = ((bf16[4,128,4,128]{3,2,1,0:T(4,128)(2,1)}), bf16[4,128,4,128]{3,2,1,0:T(4,128)(2,1)}, u32[]{:S(2)}, u32[]{:S(2)}) async-start(bf16[4,128,4,128]{3,2,1,0:T(4,128)(2,1)} %bitcast.20), calls=%async_computation.1 | async-start | bytes 1048576 | tf_op jit(solution)/shard_map/all_to_all | solution.py:60
  23.7 2.3 %copy.70 = bf16[256,1536]{0,1:T(8,128)(2,1)} copy(bf16[256,1536]{1,0:T(8,128)(2,1)} %param.8) | data formatting | bytes 1572864 | tf_op args[2]
  26.0 1.9 %copy.71 = bf16[256,12,128]{2,1,0:T(8,128)(2,1)S(1)} copy(bf16[256,12,128]{0,2,1:T(8,128)(2,1)} %bitcast.86) | data formatting | bytes 1572864 | tf_op jit(solution)/shard_map/reshape | solution.py:20
  27.9 1.1 %fusion.16 = bf16[256,8,128]{2,1,0:T(8,128)(2,1)} fusion(bf16[256,12,128]{2,1,0:T(8,128)(2,1)S(1)} %copy.71, s32[12]{0:T(128)S(1)} %add_bitcast_fusion, pred[12]{0:T(512)(128)(4,1)S(1)} %broadcast_compare_fusion), kind=kOutput, calls=%fused_computation.30 | convolution fusion | flops 6553792 | bytes 1310780 | tf_op jit(solution)/shard_map/rhd,th->rtd/dot_general | solution.py:21
  29.0 0.4 fusion.21
  29.4 0.4 fusion.19
  29.7 2.6 %gather_fusion.2 = bf16[512,4,128]{2,1,0:T(4,128)(2,1)} fusion(bf16[256,4,128]{2,1,0:T(4,128)(2,1)S(1)} %fusion.21, s32[1024]{0:T(1024)S(1)} %pad_clamp_fusion.1), kind=kCustom, calls=%fused_computation.2 | custom fusion | bytes 1050624 | tf_op jit(solution)/shard_map/gather | solution.py:58
  32.3 2.6 %gather_fusion = bf16[512,4,128]{2,1,0:T(4,128)(2,1)} fusion(bf16[256,4,128]{2,1,0:T(4,128)(2,1)S(1)} %fusion.19, s32[1024]{0:T(1024)S(1)} %pad_clamp_fusion.1), kind=kCustom, calls=%fused_computation | custom fusion | bytes 1050624 | tf_op jit(solution)/shard_map/gather | solution.py:59
  34.8 0.7 iota_compare_fusion.4
  35.5 0.1 convert_reduce_fusion
  35.6 2.7 %all-to-all-done.1 = bf16[4,128,4,128]{3,2,1,0:T(4,128)(2,1)} async-done(((bf16[4,128,4,128]{3,2,1,0:T(4,128)(2,1)}), bf16[4,128,4,128]{3,2,1,0:T(4,128)(2,1)}, u32[]{:S(2)}, u32[]{:S(2)}) %all-to-all-start.1) | async-done | bytes 524320 | tf_op jit(solution)/shard_map/all_to_all | solution.py:60
  38.3 3.5 %all-to-all-start.2 = ((bf16[4,128,4,128]{3,2,1,0:T(4,128)(2,1)}), bf16[4,128,4,128]{3,2,1,0:T(4,128)(2,1)S(1)}, u32[]{:S(2)}, u32[]{:S(2)}) async-start(bf16[4,128,4,128]{3,2,1,0:T(4,128)(2,1)} %bitcast.23), calls=%async_computation.2 | async-start | bytes 1048576 | tf_op jit(solution)/shard_map/all_to_all | solution.py:61
  41.8 0.1 select_reduce_fusion
  41.9 0.2 fusion.37
  42.0 13.7 %all-to-all-done.2 = bf16[4,128,4,128]{3,2,1,0:T(4,128)(2,1)S(1)} async-done(((bf16[4,128,4,128]{3,2,1,0:T(4,128)(2,1)}), bf16[4,128,4,128]{3,2,1,0:T(4,128)(2,1)S(1)}, u32[]{:S(2)}, u32[]{:S(2)}) %all-to-all-start.2) | async-done | bytes 524320 | tf_op jit(solution)/shard_map/all_to_all | solution.py:61
  55.7 4.1 %all-to-all-start = ((bf16[4,128,4,128]{3,2,1,0:T(4,128)(2,1)}), bf16[4,128,4,128]{3,2,1,0:T(4,128)(2,1)}, u32[]{:S(2)}, u32[]{:S(2)}) async-start(bf16[4,128,4,128]{3,2,1,0:T(4,128)(2,1)} %bitcast.16), calls=%async_computation | async-start | bytes 1048576 | tf_op jit(solution)/shard_map/all_to_all | solution.py:62
  59.9 0.6 broadcast_in_dim.46
  60.6 4.7 %broadcast_in_dim.68 = pred[8,256,512]{2,1,0:T(32,128)(4,1)} reshape(pred[8,4,64,8,64]{4,3,2,1,0:T(8,128)(4,1)S(1)} %broadcast_in_dim.46) | data formatting | bytes 2097152 | tf_op jit(solution)/shard_map/jit(_where)/broadcast_in_dim | solution.py:103
  65.3 0.3 fusion.17
  65.6 1.1 %copy.84 = bf16[4,128,4,128]{3,1,0,2:T(8,128)(2,1)S(1)} copy(bf16[4,128,4,128]{3,2,1,0:T(4,128)(2,1)} %all-to-all-done.1) | data formatting | bytes 1048576 | tf_op jit(solution)/shard_map/all_to_all | solution.py:60
  66.7 1.1 %copy.86 = bf16[4,128,4,128]{3,1,0,2:T(8,128)(2,1)S(1)} copy(bf16[4,128,4,128]{3,2,1,0:T(4,128)(2,1)} %copy-done) | data formatting | bytes 1048576 | tf_op jit(solution)/shard_map/all_to_all | solution.py:61
  67.9 3.5 %fusion.68 = (f32[4,512]{1,0:T(4,128)S(1)}, f32[4,512,512]{1,2,0:T(8,128)}) fusion(pred[512]{0:T(512)(128)(4,1)S(1)} %broadcast_bitcast_fusion, bf16[512,4,128]{2,0,1:T(8,128)(2,1)S(1)} %bitcast.88, bf16[512,4,128]{2,0,1:T(8,128)(2,1)S(1)} %bitcast.89), kind=kOutput, calls=%fused_computation.82 | convolution fusion | flops 272630272 | bytes 5251584 | tf_op jit(solution)/shard_map/sub | solution.py:15
  71.3 2.6 %all-to-all-done = bf16[4,128,4,128]{3,2,1,0:T(4,128)(2,1)} async-done(((bf16[4,128,4,128]{3,2,1,0:T(4,128)(2,1)}), bf16[4,128,4,128]{3,2,1,0:T(4,128)(2,1)}, u32[]{:S(2)}, u32[]{:S(2)}) %all-to-all-start) | async-done | bytes 524320 | tf_op jit(solution)/shard_map/all_to_all | solution.py:62
  73.9 3.0 %fusion.15 = bf16[4,16,4,8,128]{4,3,2,1,0:T(8,128)(2,1)S(1)} fusion(f32[4,512,512]{1,2,0:T(8,128)} %get-tuple-element.10, f32[4,512]{1,0:T(4,128)S(1)} %get-tuple-element.9, bf16[512,4,128]{2,1,0:T(4,128)(2,1)} %bitcast.17), kind=kOutput, calls=%fused_computation.29 | convolution fusion | flops 270794752 | bytes 5251072 | tf_op jit(solution)/shard_map/hqk,khd->qhd/dot_general | solution.py:73
  76.9 0.9 copy.120
  77.9 3.6 %all-to-all-start.3 = ((bf16[4,128,4,128]{1,3,2,0:T(8,128)(2,1)}), bf16[4,128,4,128]{1,3,2,0:T(8,128)(2,1)S(1)}, u32[]{:S(2)}, u32[]{:S(2)}) async-start(bf16[4,128,4,128]{1,3,2,0:T(8,128)(2,1)} %bitcast.82), calls=%async_computation.3 | async-start | bytes 1048576 | tf_op jit(solution)/shard_map/all_to_all | solution.py:76
  81.6 4.9 %fusion.63 = (f32[8,256]{1,0:T(8,128)S(1)}, f32[8,256,512]{2,1,0:T(8,128)}) fusion(pred[8,256,512]{2,1,0:T(32,128)(4,1)S(1)} %copy-done.1, bf16[512,8,128]{2,1,0:T(8,128)(2,1)} %all-gather.5.cloned.1.call-done, bf16[256,8,128]{2,1,0:T(8,128)(2,1)S(1)} %fusion.17), kind=kOutput, calls=%fused_computation.81 | convolution fusion | flops 272630272 | bytes 6823936 | tf_op jit(solution)/shard_map/sub | solution.py:15
  86.4 3.5 %fusion.14 = bf16[256,8,128]{0,2,1:T(8,128)(2,1)S(1)} fusion(f32[8,256,512]{2,1,0:T(8,128)} %get-tuple-element.8, f32[8,256]{1,0:T(8,128)S(1)} %get-tuple-element.7, bf16[512,8,128]{2,1,0:T(8,128)(2,1)} %all-gather.3.cloned.1.call-done), kind=kOutput, calls=%fused_computation.28 | convolution fusion | flops 270794752 | bytes 5775360 | tf_op jit(solution)/shard_map/hqk,khd->qhd/dot_general | solution.py:105
  89.9 0.3 copy.80
  90.2 0.5 fusion.57
  90.7 4.6 %all-to-all-done.3 = bf16[4,128,4,128]{1,3,2,0:T(8,128)(2,1)S(1)} async-done(((bf16[4,128,4,128]{1,3,2,0:T(8,128)(2,1)}), bf16[4,128,4,128]{1,3,2,0:T(8,128)(2,1)S(1)}, u32[]{:S(2)}, u32[]{:S(2)}) %all-to-all-start.3) | async-done | bytes 524320 | tf_op jit(solution)/shard_map/all_to_all | solution.py:76
  95.3 0.3 copy.89
  95.6 1.0 gather_fusion.3
  96.6 0.6 fusion.11
  97.2 0.9 copy.90
  98.1 1.2 %copy.91 = bf16[256,1536]{1,0:T(8,128)(2,1)} copy(bf16[256,1536]{0,1:T(8,128)(2,1)S(1)} %bitcast.83) | data formatting | bytes 1572864 | tf_op jit(solution)/shard_map/reshape | solution.py:117
  (26 shorter events, 0.2 us)
Async XLA Ops:
  6.5 75.0 %all-gather.5.cloned.1.call-start = ((), (), s32[]{:S(2)}) async-start(), calls=%async_computation.5 | async-start | bytes 1572864 | tf_op jit(solution)/shard_map/all_gather | solution.py:86
  7.5 6.0 %copy-start.3 = (s32[1,4]{1,0:T(1,128)S(1)}, s32[1,4]{1,0:T(1,128)}, u32[]{:S(2)}) copy-start(s32[1,4]{1,0:T(1,128)} %param.10) | copy-start | bytes 52
  17.4 20.9 %all-to-all-start.1 = ((bf16[4,128,4,128]{3,2,1,0:T(4,128)(2,1)}), bf16[4,128,4,128]{3,2,1,0:T(4,128)(2,1)}, u32[]{:S(2)}, u32[]{:S(2)}) async-start(bf16[4,128,4,128]{3,2,1,0:T(4,128)(2,1)} %bitcast.20), calls=%async_computation.1 | async-start | bytes 1048576 | tf_op jit(solution)/shard_map/all_to_all | solution.py:60
  23.7 62.7 %all-gather.3.cloned.1.call-start = ((), (), s32[]{:S(2)}) async-start(), calls=%async_computation.4 | async-start | bytes 1572864 | tf_op jit(solution)/shard_map/all_gather | solution.py:87
  27.9 14.0 %copy-start.2 = (s32[12,8,8]{0,2,1:T(8,128)S(1)}, s32[12,8,8]{0,2,1:T(8,128)}, u32[]{:S(2)}) copy-start(s32[12,8,8]{0,2,1:T(8,128)} %param.9) | copy-start | bytes 9220
  38.3 17.4 %all-to-all-start.2 = ((bf16[4,128,4,128]{3,2,1,0:T(4,128)(2,1)}), bf16[4,128,4,128]{3,2,1,0:T(4,128)(2,1)S(1)}, u32[]{:S(2)}, u32[]{:S(2)}) async-start(bf16[4,128,4,128]{3,2,1,0:T(4,128)(2,1)} %bitcast.23), calls=%async_computation.2 | async-start | bytes 1048576 | tf_op jit(solution)/shard_map/all_to_all | solution.py:61
  55.7 4.2 %copy-start = (bf16[4,128,4,128]{3,2,1,0:T(4,128)(2,1)}, bf16[4,128,4,128]{3,2,1,0:T(4,128)(2,1)S(1)}, u32[]{:S(2)}) copy-start(bf16[4,128,4,128]{3,2,1,0:T(4,128)(2,1)S(1)} %all-to-all-done.2) | copy-start | bytes 1572868
  55.7 18.2 %all-to-all-start = ((bf16[4,128,4,128]{3,2,1,0:T(4,128)(2,1)}), bf16[4,128,4,128]{3,2,1,0:T(4,128)(2,1)}, u32[]{:S(2)}, u32[]{:S(2)}) async-start(bf16[4,128,4,128]{3,2,1,0:T(4,128)(2,1)} %bitcast.16), calls=%async_computation | async-start | bytes 1048576 | tf_op jit(solution)/shard_map/all_to_all | solution.py:62
  73.9 7.6 %copy-start.1 = (pred[8,256,512]{2,1,0:T(32,128)(4,1)S(1)}, pred[8,256,512]{2,1,0:T(32,128)(4,1)}, u32[]{:S(2)}) copy-start(pred[8,256,512]{2,1,0:T(32,128)(4,1)} %broadcast_in_dim.68) | copy-start | bytes 3145732
  77.9 17.4 %all-to-all-start.3 = ((bf16[4,128,4,128]{1,3,2,0:T(8,128)(2,1)}), bf16[4,128,4,128]{1,3,2,0:T(8,128)(2,1)S(1)}, u32[]{:S(2)}, u32[]{:S(2)}) async-start(bf16[4,128,4,128]{1,3,2,0:T(8,128)(2,1)} %bitcast.82), calls=%async_computation.3 | async-start | bytes 1048576 | tf_op jit(solution)/shard_map/all_to_all | solution.py:76
Sparse Core Ops, SparseCore 0:
  11.2 11.7 all-gather.4
  29.1 10.4 all-gather.2
where the time goes:
time: 107 us; the launch traced here: 106 us
  local copies, waits for them, and re-layouts  28.9 us (27%)
  waiting for transfers between devices  23.6 us (22%)
  matrix products  19.5 us (18%)
  starting transfers between devices  17.6 us (16%)
  between operations  13.6 us (13%)
  other arithmetic  2.82 us (3%)
    all_to_all x1, waiting for transfers between devices, local(): lax.all_to_all(send_keys, 'frames', split_axis=0, concat_axis=0, tiled=True)  13.7 us
    sub x2, matrix products, softmax_weights(): raised = jnp.exp(scores - highest)  8.31 us
    all_to_all x1, starting transfers between devices, local(): lax.all_to_all(send_query, 'frames', split_axis=0, concat_axis=0, tiled=T...  6.32 us
    broadcast_in_dim x2, local copies, waits for them, and re-layouts, local(): shaped = jnp.where(mask_rows[:, :, None, :, None], shaped, MASKED_SCORE)  5.33 us
    unnamed x11, local copies, waits for them, and re-layouts  5.12 us
    all_to_all x1, waiting for transfers between devices, local(): lax.all_to_all(tile_out.reshape(frame_count, slot_count, item_count, HD),...  4.59 us
    all_to_all x1, starting transfers between devices, local(): lax.all_to_all(send_values, 'frames', split_axis=0, concat_axis=0, tiled=...  4.14 us
    reshape x3, local copies, waits for them, and re-layouts, select_heads(): head_grid = token_rows.reshape(token_rows.shape[0], -1, HD)  3.93 us
  transfers between devices with their start and end apart: 6, of which 4 were waited for; matrix products, arithmetic and copies ran while one was open for 40% of the time, Pallas kernels for 0%

commit v1 on v0

v1 whole, which is shorter than its diff:
```python
import functools
import math

import jax
import jax.numpy as jnp
from jax import lax
from jax.experimental import pallas as pl
from jax.experimental.pallas import tpu as pltpu
from jax.sharding import PartitionSpec as P

HD = 128
BLK = 64
MASKED_SCORE = -1e30
EXP2_SCALE = HD ** (-0.5) * math.log2(math.e)
MESH = pl.DeviceIdType.MESH


def softmax_weights(scores):
    highest = jnp.max(scores, axis=-1, keepdims=True)
    raised = jnp.exp(scores - highest)
    return (raised / jnp.sum(raised, axis=-1, keepdims=True)).astype(jnp.bfloat16)


def tile_numbers(positions, ends):
    return sum((positions >= end).astype(jnp.int32) for end in ends)


def plain(query, key_proj, value, block_mask, tile_sizes, temporal_ids):
    rows, heads_here = query.shape[0], block_mask.shape[0]
    temp_here, frame_blocks = temporal_ids.shape[0], block_mask.shape[1]
    score_scale = HD ** (-0.5)
    local_ids = temporal_ids - lax.axis_index("heads") * heads_here
    pick = local_ids[:, None] == jnp.arange(heads_here, dtype=jnp.int32)[None, :]

    def grid(rows_of):
        return rows_of.reshape(rows_of.shape[0], heads_here, HD)

    def chosen(rows_of):
        return jnp.einsum(
            "rhd,th->rtd", grid(rows_of), pick.astype(jnp.bfloat16), preferred_element_type=jnp.float32
        ).astype(jnp.bfloat16)

    temp_query = chosen(query)
    temp_keys = lax.all_gather(chosen(key_proj), "frames", axis=0, tiled=True)
    temp_values = lax.all_gather(chosen(value), "frames", axis=0, tiled=True)
    tile_len = tile_sizes[0]
    index = jnp.arange(tile_len.shape[0], dtype=jnp.int32)
    ends = jnp.sum(jnp.where(index[None, :] <= index[:, None], tile_len[None, :], 0), axis=1)
    positions = jnp.arange(rows, dtype=jnp.int32)
    tile_of = jnp.sum((positions[:, None] >= ends[None, :]).astype(jnp.int32), axis=1)
    scores = (
        jnp.einsum("qhd,khd->hqk", temp_query, temp_keys, preferred_element_type=jnp.float32) * score_scale
    )
    shaped = scores.reshape(temp_here, rows, -1, rows)
    same = tile_of[:, None] == tile_of[None, :]
    shaped = jnp.where(same[None, :, None, :], shaped, MASKED_SCORE)
    weights = softmax_weights(shaped.reshape(scores.shape))
    temp_out = jnp.einsum(
        "hqk,khd->qhd", weights, temp_values, preferred_element_type=jnp.float32
    ).astype(jnp.bfloat16)

    keys = grid(lax.all_gather(key_proj, "rep", axis=0, tiled=True))
    values = grid(lax.all_gather(value, "rep", axis=0, tiled=True))
    query_blocks = rows // BLK
    mask_rows = lax.dynamic_slice_in_dim(block_mask, lax.axis_index("rep") * query_blocks, query_blocks, 1)
    scores = jnp.einsum("qhd,khd->hqk", grid(query), keys, preferred_element_type=jnp.float32) * score_scale
    shaped = scores.reshape(heads_here, query_blocks, BLK, frame_blocks, BLK)
    shaped = jnp.where(mask_rows[:, :, None, :, None] == 1, shaped, MASKED_SCORE)
    weights = softmax_weights(shaped.reshape(scores.shape))
    spat_out = jnp.einsum("hqk,khd->qhd", weights, values, preferred_element_type=jnp.float32)
    spread = jnp.einsum(
        "rtd,th->rhd", temp_out, pick.astype(jnp.bfloat16), preferred_element_type=jnp.float32
    )
    is_temp = jnp.any(pick, axis=0)
    combined = jnp.where(is_temp[None, :, None], spread, spat_out)
    return combined.astype(jnp.bfloat16).reshape(rows, heads_here * HD)


def across(me, step):
    if step == 0:
        return me
    if step == 1:
        return me + 1 - 2 * lax.rem(me, 2)
    if step == 2:
        return lax.rem(me + 2, 4)
    return 3 - me


def weigh(scores, values):
    highest = jnp.max(scores, axis=-1, keepdims=True)
    raised = jnp.exp2(scores - highest)
    total = jnp.sum(raised, axis=-1, keepdims=True)
    out = jnp.dot(raised.astype(jnp.bfloat16), values, preferred_element_type=jnp.float32)
    return (out / total).astype(jnp.bfloat16)


def products(left, right):
    return lax.dot_general(left, right, (((1,), (1,)), ((), ())), preferred_element_type=jnp.float32)


def kernel(
    heads, ids, tiles, mask, q_hbm, k_hbm, v_hbm, out,
    q_own, k_own, v_own, q_heads, k_heads, v_heads, k_peer, v_peer, q_send, k_send, v_send, q_tile, k_tile, v_tile, o_send,
    held, mask_rows, tile_bias, load_sem, pair_send, pair_recv, z_send, z_recv,
):
    rows = q_own.shape[0]
    frames = 4
    blocks = rows // BLK
    me, half = lax.axis_index("frames"), lax.axis_index("rep")
    loads = [
        pltpu.make_async_copy(src, dst, load_sem.at[i])
        for i, (src, dst) in enumerate(((k_hbm, k_own), (v_hbm, v_own), (q_hbm, q_own)))
    ]
    for load in loads:
        load.start()
    barrier = pltpu.get_barrier_semaphore()
    for step in (1, 2, 3):
        pl.semaphore_signal(barrier, inc=1, device_id={"frames": across(me, step)}, device_id_type=MESH)
    pl.semaphore_signal(barrier, inc=1, device_id={"rep": 1 - half}, device_id_type=MESH)
    local_ids = [lax.rem(ids[across(me, step)], heads) for step in range(frames)]

    def pick(source, by_head, own_tile, sends):
        for h in range(heads):
            by_head[h] = source[:, h * HD : (h + 1) * HD]
        for step in (2, 3, 1, 0):
            if step:
                sends[step] = by_head[local_ids[step]]
            else:
                own_tile[pl.ds(0, rows), :] = by_head[local_ids[step]]

    def z_copy(kind, step, src, dst):
        return pltpu.make_async_remote_copy(
            src_ref=src, dst_ref=dst, send_sem=z_send.at[kind, step], recv_sem=z_recv.at[kind, step],
            device_id={"frames": across(me, step)}, device_id_type=MESH,
        )

    def pair_copy(i, src, dst):
        return pltpu.make_async_remote_copy(
            src_ref=src, dst_ref=dst, send_sem=pair_send.at[i], recv_sem=pair_recv.at[i],
            device_id={"rep": 1 - half}, device_id_type=MESH,
        )

    pairs = [pair_copy(0, k_hbm, k_peer), pair_copy(1, v_hbm, v_peer)]
    sent = []
    for kind, (source, by_head, own_tile, sends) in enumerate(
        ((k_own, k_heads, k_tile, k_send), (v_own, v_heads, v_tile, v_send), (q_own, q_heads, q_tile, q_send))
    ):
        loads[kind].wait()
        pick(source, by_head, own_tile, sends)
        if kind == 0:
            pl.semaphore_wait(barrier, frames)
        for step in (2, 3, 1):
            copy = z_copy(kind, step, sends.at[step], own_tile.at[pl.ds(step * rows, rows)])
            copy.start()
            sent.append(copy)
        if kind < 2:
            pairs[kind].start()

    ends, end = [], 0
    for j in range(frames):
        end = end + tiles[0, j]
        ends.append(end)
    down = lax.broadcasted_iota(jnp.int32, (rows, rows), 0)
    along = lax.broadcasted_iota(jnp.int32, (rows, rows), 1)
    tile_bias[...] = jnp.where(tile_numbers(down, ends) == tile_numbers(along, ends), 0.0, MASKED_SCORE)

    key_block = lax.rem(lax.broadcasted_iota(jnp.int32, (2 * blocks, 2 * rows), 1) // BLK + blocks * half, 2 * blocks)
    lies = (key_block == lax.broadcasted_iota(jnp.int32, (2 * blocks, 2 * rows), 0)).astype(jnp.bfloat16)
    flat_mask = mask[...].reshape(heads * 2 * blocks, 2 * blocks).astype(jnp.float32).astype(jnp.bfloat16)
    seen = jnp.dot(flat_mask, lies, preferred_element_type=jnp.float32)
    mask_rows[...] = jnp.where(seen > 0.5, 0.0, MASKED_SCORE)

    for pair in pairs:
        pair.wait()

    def spatial(h, carry):
        columns = pl.ds(pl.multiple_of(h * HD, HD), HD)
        bias = mask_rows[pl.ds(pl.multiple_of(h * 2 * blocks, 2 * blocks), 2 * blocks), :]
        bias = jnp.where(half == 0, bias[:blocks], bias[blocks:])
        bias = jnp.concatenate(
            [jnp.broadcast_to(bias[i : i + 1], (BLK, 2 * rows)) for i in range(blocks)], axis=0
        )
        q = q_heads[h]
        scores = jnp.concatenate(
            [products(q, k_heads[h]), products(q, k_peer[:, columns])], axis=1
        )
        values = jnp.concatenate([v_heads[h], v_peer[:, columns]], axis=0)
        held[h] = weigh(scores * EXP2_SCALE + bias, values)
        return carry

    lax.fori_loop(0, heads, spatial, 0)

    for copy in sent[:6]:
        copy.wait()
    returned = []
    for step in (2, 3, 1, 0):
        if step:
            sent[6 + (2, 3, 1).index(step)].wait()
        scores = products(q_tile[pl.ds(step * rows, rows), :], k_tile[...]) * EXP2_SCALE
        bias = jnp.concatenate([tile_bias[...]] * frames, axis=1)
        result = weigh(scores + bias, v_tile[...])
        if step:
            o_send[step] = result
            copy = z_copy(3, step, o_send.at[step], held.at[heads + step])
            copy.start()
            returned.append(copy)
        else:
            held[heads] = result
    for copy in returned:
        copy.wait()
    for h in range(heads):
        slot = h
        for step in range(frames):
            slot = jnp.where(local_ids[step] == h, heads + step, slot)
        out[:, h * HD : (h + 1) * HD] = held[slot]


def fused(query, key_proj, value, block_mask, tile_sizes, temporal_ids):
    rows, width = query.shape
    heads = block_mask.shape[0]
    whole = pltpu.VMEM((rows, width), jnp.bfloat16)
    parted = pltpu.VMEM((heads, rows, HD), jnp.bfloat16)
    tiles = pltpu.VMEM((4, rows, HD), jnp.bfloat16)
    flat = pltpu.VMEM((4 * rows, HD), jnp.bfloat16)
    smem, vmem = pl.BlockSpec(memory_space=pltpu.SMEM), pl.BlockSpec(memory_space=pltpu.VMEM)
    anywhere = pl.BlockSpec(memory_space=pl.ANY)
    return pl.pallas_call(
        functools.partial(kernel, heads),
        out_shape=jax.ShapeDtypeStruct((rows, width), jnp.bfloat16),
        in_specs=[smem, smem, vmem, anywhere, anywhere, anywhere],
        out_specs=vmem,
        scratch_shapes=[
            whole, whole, whole, parted, parted, parted, whole, whole, tiles, tiles, tiles, flat, flat, flat, tiles,
            pltpu.VMEM((heads + 4, rows, HD), jnp.bfloat16),
            pltpu.VMEM((heads * 2 * rows // BLK, 2 * rows), jnp.float32),
            pltpu.VMEM((rows, rows), jnp.float32),
            pltpu.SemaphoreType.DMA((3,)),
            pltpu.SemaphoreType.DMA((2,)),
            pltpu.SemaphoreType.DMA((2,)),
            pltpu.SemaphoreType.DMA((4, 4)),
            pltpu.SemaphoreType.DMA((4, 4)),
        ],
        compiler_params=pltpu.CompilerParams(
            collective_id=0, has_side_effects=True, vmem_limit_bytes=40 * 2**20
        ),
    )(temporal_ids, tile_sizes, block_mask, query, key_proj, value)


def solution(mesh):
    def local(query, key_proj, value, block_mask, tile_sizes, temporal_ids):
        by_head = mesh.shape["frames"] == temporal_ids.shape[0] == 4 and mesh.shape["rep"] == 2
        chosen = fused if by_head else plain
        return chosen(query, key_proj, value, block_mask, tile_sizes, temporal_ids)

    in_specs = (
        P(("groups", "frames", "rep"), "heads"),
        P(("groups", "frames", "rep"), "heads"),
        P(("groups", "frames", "rep"), "heads"),
        P("heads", None, None),
        P("rep", None),
        P("heads"),
    )
    out_specs = P(("groups", "frames", "rep"), "heads")
    return jax.shard_map(local, mesh=mesh, in_specs=in_specs, out_specs=out_specs, check_vma=False)
```

time: 107 us -> 35.3 us (0.33)
  Pallas kernels: 0 us -> 29.8 us
  local copies, waits for them, and re-layouts: 28.9 us -> 5.19 us
  waiting for transfers between devices: 23.6 us -> 0 us
  matrix products: 19.5 us -> 0 us
  starting transfers between devices: 17.6 us -> 0 us
  between operations: 13.6 us -> 0.03 us
  other arithmetic: 2.82 us -> 0 us
    pallas_call x0 -> x1, Pallas kernels: none -> 29.8 us  [fused(): pl.pallas_call(functools.partial(kernel, heads), out_shape=jax.ShapeDtype...]
    all_to_all x4 -> x0, waiting for transfers between devices: 23.6 us -> none  [the longest x1 13.7 us: local(): lax.all_to_all(send_keys, 'frames', split_axis=0, concat_axis=0, tiled=True)]
    all_to_all x4 -> x0, starting transfers between devices: 17.6 us -> none  [the longest x1 6.32 us: local(): lax.all_to_all(send_query, 'frames', split_axis=0, concat_axis=0, tiled=T...]
    dot_general x11 -> x0, matrix products: 11.2 us -> none  [the longest x6 3.5 us: select_heads(): jnp.einsum('rhd,th->rtd', head_grid, picker.astype(jnp.bfloat16), preferr...]
    gather x4 -> x0, local copies, waits for them, and re-layouts: 8.63 us -> none  [the longest x1 2.55 us: local(): send_keys = select_heads(key_proj, pick_temp)[source_rows]]
    sub x2 -> x0, matrix products: 8.31 us -> none  [softmax_weights(): raised = jnp.exp(scores - highest)]
    reshape x5 -> x0, local copies, waits for them, and re-layouts: 6.04 us -> none  [the longest x3 3.93 us: select_heads(): head_grid = token_rows.reshape(token_rows.shape[0], -1, HD)]
    broadcast_in_dim x3 -> x0, local copies, waits for them, and re-layouts: 5.34 us -> none  [the longest x2 5.33 us: local(): shaped = jnp.where(mask_rows[:, :, None, :, None], shaped, MASKED_SCORE)]
  transfers between devices with their start and end apart: 6 -> 0, of which waited for: 4 -> 0; matrix products, arithmetic and copies ran while one was open for 40% -> 0% of each run, Pallas kernels for 0% -> 0%
where the time goes in v1:
time: 35.3 us; the launch traced here: 35 us
  Pallas kernels  29.8 us (84%)
  local copies, waits for them, and re-layouts  5.19 us (15%)
    pallas_call x1, Pallas kernels, fused(): pl.pallas_call(functools.partial(kernel, heads), out_shape=jax.ShapeDtype...  29.8 us
    unnamed x12, local copies, waits for them, and re-layouts  5.19 us

profile of v1, /device:TPU:0, one launch (start us, length us, event | category | flops | bytes accessed | tf_op | source)
XLA Modules:
  0.0 35.0 jit_solution(1192703487659334926)
XLA Ops:
  0.0 0.0 copy-start.3
  0.0 0.0 copy-start.4
  0.0 0.9 %copy.7.mask = s32[12,8,8]{2,1,0:T(8,128)S(1)} copy(s32[12,8,8]{0,2,1:T(8,128)} %param.9) | data formatting | bytes 6144 | tf_op args[3]
  0.9 0.0 copy-done.3
  0.9 0.0 copy-done.4
  0.9 0.0 copy-start
  0.9 1.1 %copy-done = bf16[256,1536]{1,0:T(8,128)(2,1)S(1)} copy-done((bf16[256,1536]{1,0:T(8,128)(2,1)S(1)}, bf16[256,1536]{1,0:T(8,128)(2,1)}, u32[]{:S(2)}) %copy-start) | copy-done | bytes 786456
  2.1 0.0 copy-start.1
  2.1 1.1 %copy-done.1 = bf16[256,1536]{1,0:T(8,128)(2,1)S(1)} copy-done((bf16[256,1536]{1,0:T(8,128)(2,1)S(1)}, bf16[256,1536]{1,0:T(8,128)(2,1)}, u32[]{:S(2)}) %copy-start.1) | copy-done | bytes 786456
  3.2 0.0 copy-start.2
  3.2 1.1 %copy-done.2 = bf16[256,1536]{1,0:T(8,128)(2,1)S(1)} copy-done((bf16[256,1536]{1,0:T(8,128)(2,1)S(1)}, bf16[256,1536]{1,0:T(8,128)(2,1)}, u32[]{:S(2)}) %copy-start.2) | copy-done | bytes 786456
  4.3 29.8 %shard_map.64 = bf16[256,1536]{1,0:T(8,128)(2,1)S(1)} custom-call(s32[4]{0:T(128)S(1)} %copy-done.3, s32[1,4]{1,0:T(1,128)S(1)} %copy-done.4, s32[12,8,8]{2,1,0:T(8,128)S(1)} %copy.7.mask, bf16[256,1536]{1,0:T(8,128)(2,1)S(1)} %copy-done, bf16[256,1536]{1,0:T(8,128)(2,1)S(1)} %copy-done.1, bf16[256,1536]{1,0:T(8,128)(2,1)S(1)} %copy-done.2), custom_call_target="tpu_custom_call" | custom-call | tf_op jit(solution)/shard_map/pallas_call | solution.py:227
  34.1 0.9 %copy.9 = bf16[256,1536]{1,0:T(8,128)(2,1)} copy(bf16[256,1536]{1,0:T(8,128)(2,1)S(1)} %shard_map.64) | data formatting | bytes 1572864
Async XLA Ops:
  0.0 0.9 %copy-start.3 = (s32[4]{0:T(128)S(1)}, s32[4]{0:T(128)}, u32[]{:S(2)}) copy-start(s32[4]{0:T(128)} %ids.1) | copy-start | bytes 52
  0.0 0.9 %copy-start.4 = (s32[1,4]{1,0:T(1,128)S(1)}, s32[1,4]{1,0:T(1,128)}, u32[]{:S(2)}) copy-start(s32[1,4]{1,0:T(1,128)} %tiles.1) | copy-start | bytes 52
  0.9 1.1 %copy-start = (bf16[256,1536]{1,0:T(8,128)(2,1)S(1)}, bf16[256,1536]{1,0:T(8,128)(2,1)}, u32[]{:S(2)}) copy-start(bf16[256,1536]{1,0:T(8,128)(2,1)} %q_hbm.1) | copy-start | bytes 2359300
  2.1 1.1 %copy-start.1 = (bf16[256,1536]{1,0:T(8,128)(2,1)S(1)}, bf16[256,1536]{1,0:T(8,128)(2,1)}, u32[]{:S(2)}) copy-start(bf16[256,1536]{1,0:T(8,128)(2,1)} %k_hbm.1) | copy-start | bytes 2359300
  3.2 1.1 %copy-start.2 = (bf16[256,1536]{1,0:T(8,128)(2,1)S(1)}, bf16[256,1536]{1,0:T(8,128)(2,1)}, u32[]{:S(2)}) copy-start(bf16[256,1536]{1,0:T(8,128)(2,1)} %v_hbm.1) | copy-start | bytes 2359300

commit v2 on v1

--- a/solution.py
+++ b/solution.py
@@ -99,7 +99,7 @@
 
 
 def kernel(
-    heads, ids, tiles, mask, q_hbm, k_hbm, v_hbm, out,
+    heads, ids_hbm, tiles_hbm, mask_hbm, q_hbm, k_hbm, v_hbm, out, ids, tiles, mask,
     q_own, k_own, v_own, q_heads, k_heads, v_heads, k_peer, v_peer, q_send, k_send, v_send, q_tile, k_tile, v_tile, o_send,
     held, mask_rows, tile_bias, load_sem, pair_send, pair_recv, z_send, z_recv,
 ):
@@ -109,14 +109,17 @@
     me, half = lax.axis_index("frames"), lax.axis_index("rep")
     loads = [
         pltpu.make_async_copy(src, dst, load_sem.at[i])
-        for i, (src, dst) in enumerate(((k_hbm, k_own), (v_hbm, v_own), (q_hbm, q_own)))
+        for i, (src, dst) in enumerate(
+            ((k_hbm, k_own), (v_hbm, v_own), (q_hbm, q_own), (ids_hbm, ids), (tiles_hbm, tiles), (mask_hbm, mask))
+        )
     ]
-    for load in loads:
-        load.start()
+    for i in (3, 0, 1, 2, 4, 5):
+        loads[i].start()
     barrier = pltpu.get_barrier_semaphore()
     for step in (1, 2, 3):
         pl.semaphore_signal(barrier, inc=1, device_id={"frames": across(me, step)}, device_id_type=MESH)
     pl.semaphore_signal(barrier, inc=1, device_id={"rep": 1 - half}, device_id_type=MESH)
+    loads[3].wait()
     local_ids = [lax.rem(ids[across(me, step)], heads) for step in range(frames)]
 
     def pick(source, by_head, own_tile, sends):
@@ -141,7 +144,7 @@
         )
 
     pairs = [pair_copy(0, k_hbm, k_peer), pair_copy(1, v_hbm, v_peer)]
-    sent = []
+    sent = {}
     for kind, (source, by_head, own_tile, sends) in enumerate(
         ((k_own, k_heads, k_tile, k_send), (v_own, v_heads, v_tile, v_send), (q_own, q_heads, q_tile, q_send))
     ):
@@ -152,10 +155,12 @@
         for step in (2, 3, 1):
             copy = z_copy(kind, step, sends.at[step], own_tile.at[pl.ds(step * rows, rows)])
             copy.start()
-            sent.append(copy)
+            sent[kind, step] = copy
         if kind < 2:
             pairs[kind].start()
 
+    loads[4].wait()
+    loads[5].wait()
     ends, end = [], 0
     for j in range(frames):
         end = end + tiles[0, j]
@@ -165,20 +170,21 @@
     tile_bias[...] = jnp.where(tile_numbers(down, ends) == tile_numbers(along, ends), 0.0, MASKED_SCORE)
 
     key_block = lax.rem(lax.broadcasted_iota(jnp.int32, (2 * blocks, 2 * rows), 1) // BLK + blocks * half, 2 * blocks)
-    lies = (key_block == lax.broadcasted_iota(jnp.int32, (2 * blocks, 2 * rows), 0)).astype(jnp.bfloat16)
-    flat_mask = mask[...].reshape(heads * 2 * blocks, 2 * blocks).astype(jnp.float32).astype(jnp.bfloat16)
-    seen = jnp.dot(flat_mask, lies, preferred_element_type=jnp.float32)
-    mask_rows[...] = jnp.where(seen > 0.5, 0.0, MASKED_SCORE)
+    lies = (key_block == lax.broadcasted_iota(jnp.int32, (2 * blocks, 2 * rows), 0)).astype(jnp.float32)
+    for i in range(blocks):
+        seen = lax.dot_general(
+            mask[half * blocks + i].astype(jnp.float32), lies, (((0,), (0,)), ((), ())),
+            preferred_element_type=jnp.float32,
+        )
+        mask_rows[i] = jnp.where(seen > 0.5, 0.0, MASKED_SCORE)
 
     for pair in pairs:
         pair.wait()
 
     def spatial(h, carry):
         columns = pl.ds(pl.multiple_of(h * HD, HD), HD)
-        bias = mask_rows[pl.ds(pl.multiple_of(h * 2 * blocks, 2 * blocks), 2 * blocks), :]
-        bias = jnp.where(half == 0, bias[:blocks], bias[blocks:])
         bias = jnp.concatenate(
-            [jnp.broadcast_to(bias[i : i + 1], (BLK, 2 * rows)) for i in range(blocks)], axis=0
+            [jnp.broadcast_to(mask_rows[i, pl.ds(h, 1), :], (BLK, 2 * rows)) for i in range(blocks)], axis=0
         )
         q = q_heads[h]
         scores = jnp.concatenate(
@@ -190,12 +196,13 @@
 
     lax.fori_loop(0, heads, spatial, 0)
 
-    for copy in sent[:6]:
-        copy.wait()
+    for step in (2, 3, 1):
+        sent[0, step].wait()
+        sent[1, step].wait()
     returned = []
     for step in (2, 3, 1, 0):
         if step:
-            sent[6 + (2, 3, 1).index(step)].wait()
+            sent[2, step].wait()
         scores = products(q_tile[pl.ds(step * rows, rows), :], k_tile[...]) * EXP2_SCALE
         bias = jnp.concatenate([tile_bias[...]] * frames, axis=1)
         result = weigh(scores + bias, v_tile[...])
@@ -222,19 +229,22 @@
     parted = pltpu.VMEM((heads, rows, HD), jnp.bfloat16)
     tiles = pltpu.VMEM((4, rows, HD), jnp.bfloat16)
     flat = pltpu.VMEM((4 * rows, HD), jnp.bfloat16)
-    smem, vmem = pl.BlockSpec(memory_space=pltpu.SMEM), pl.BlockSpec(memory_space=pltpu.VMEM)
-    anywhere = pl.BlockSpec(memory_space=pl.ANY)
+    turned = block_mask.transpose(1, 2, 0)
+    operands = (temporal_ids, tile_sizes, turned, query, key_proj, value)
     return pl.pallas_call(
         functools.partial(kernel, heads),
-        out_shape=jax.ShapeDtypeStruct((rows, width), jnp.bfloat16),
-        in_specs=[smem, smem, vmem, anywhere, anywhere, anywhere],
-        out_specs=vmem,
+        out_shape=pltpu.VMEM((rows, width), jnp.bfloat16),
+        in_specs=[pl.BlockSpec(memory_space=pltpu.HBM)] * len(operands),
+        out_specs=pl.BlockSpec(memory_space=pltpu.VMEM),
         scratch_shapes=[
+            pltpu.SMEM(temporal_ids.shape, jnp.int32),
+            pltpu.SMEM(tile_sizes.shape, jnp.int32),
+            pltpu.VMEM(turned.shape, jnp.int32),
             whole, whole, whole, parted, parted, parted, whole, whole, tiles, tiles, tiles, flat, flat, flat, tiles,
             pltpu.VMEM((heads + 4, rows, HD), jnp.bfloat16),
-            pltpu.VMEM((heads * 2 * rows // BLK, 2 * rows), jnp.float32),
+            pltpu.VMEM((rows // BLK, heads, 2 * rows), jnp.float32),
             pltpu.VMEM((rows, rows), jnp.float32),
-            pltpu.SemaphoreType.DMA((3,)),
+            pltpu.SemaphoreType.DMA((6,)),
             pltpu.SemaphoreType.DMA((2,)),
             pltpu.SemaphoreType.DMA((2,)),
             pltpu.SemaphoreType.DMA((4, 4)),
@@ -243,7 +253,7 @@
         compiler_params=pltpu.CompilerParams(
             collective_id=0, has_side_effects=True, vmem_limit_bytes=40 * 2**20
         ),
-    )(temporal_ids, tile_sizes, block_mask, query, key_proj, value)
+    )(*(pltpu.with_memory_space_constraint(x, pltpu.HBM) for x in operands))
 
 
 def solution(mesh):

time: 35.3 us -> 30.5 us (0.86)
  local copies, waits for them, and re-layouts: 5.19 us -> 0.88 us
    unnamed x12 -> x1, local copies, waits for them, and re-layouts: 5.19 us -> 0.88 us
where the time goes in v2:
time: 30.5 us; the launch traced here: 30.4 us
  Pallas kernels  29.5 us (97%)
  local copies, waits for them, and re-layouts  0.88 us (3%)
    pallas_call x1, Pallas kernels, fused(): pl.pallas_call(functools.partial(kernel, heads), out_shape=pltpu.VMEM((ro...  29.5 us
    unnamed x1, local copies, waits for them, and re-layouts  0.88 us

profile of v2, /device:TPU:0, one launch (start us, length us, event | category | flops | bytes accessed | tf_op | source)
XLA Modules:
  0.0 30.4 jit_solution(10252255483102756079)
XLA Ops:
  0.0 29.5 %shard_map.64 = bf16[256,1536]{1,0:T(8,128)(2,1)S(1)} custom-call(s32[4]{0:T(128)} %ids_hbm.1, s32[1,4]{1,0:T(1,128)} %tiles_hbm.1, s32[8,8,12]{2,1,0:T(8,128)} %bitcast.1, bf16[256,1536]{1,0:T(8,128)(2,1)} %q_hbm.1, bf16[256,1536]{1,0:T(8,128)(2,1)} %k_hbm.1, bf16[256,1536]{1,0:T(8,128)(2,1)} %v_hbm.1), custom_call_target="tpu_custom_call" | custom-call | tf_op jit(solution)/shard_map/pallas_call | solution.py:234
  29.5 0.9 %copy.8 = bf16[256,1536]{1,0:T(8,128)(2,1)} copy(bf16[256,1536]{1,0:T(8,128)(2,1)S(1)} %shard_map.64) | data formatting | bytes 1572864

commit v3 on v2

--- a/solution.py
+++ b/solution.py
@@ -113,7 +113,13 @@
             ((k_hbm, k_own), (v_hbm, v_own), (q_hbm, q_own), (ids_hbm, ids), (tiles_hbm, tiles), (mask_hbm, mask))
         )
     ]
-    for i in (3, 0, 1, 2, 4, 5):
+    side = heads // 2 * HD
+    loads[0] = pltpu.make_async_copy(k_hbm.at[:, :side], k_own.at[:, :side], load_sem.at[0])
+    later_keys = pltpu.make_async_copy(k_hbm.at[:, side:], k_own.at[:, side:], load_sem.at[6])
+    loads[3].start()
+    loads[0].start()
+    later_keys.start()
+    for i in (1, 2, 4, 5):
         loads[i].start()
     barrier = pltpu.get_barrier_semaphore()
     for step in (1, 2, 3):
@@ -124,6 +130,8 @@
 
     def pick(source, by_head, own_tile, sends):
         for h in range(heads):
+            if source is k_own and h == heads // 2:
+                later_keys.wait()
             by_head[h] = source[:, h * HD : (h + 1) * HD]
         for step in (2, 3, 1, 0):
             if step:
@@ -244,7 +252,7 @@
             pltpu.VMEM((heads + 4, rows, HD), jnp.bfloat16),
             pltpu.VMEM((rows // BLK, heads, 2 * rows), jnp.float32),
             pltpu.VMEM((rows, rows), jnp.float32),
-            pltpu.SemaphoreType.DMA((6,)),
+            pltpu.SemaphoreType.DMA((7,)),
             pltpu.SemaphoreType.DMA((2,)),
             pltpu.SemaphoreType.DMA((2,)),
             pltpu.SemaphoreType.DMA((4, 4)),

time: 30.5 us -> 30.4 us (level)
  no operation moved by 1% of the time
where the time goes in v3:
time: 30.4 us; the launch traced here: 30.3 us
  Pallas kernels  29.4 us (97%)
  local copies, waits for them, and re-layouts  0.88 us (3%)
    pallas_call x1, Pallas kernels, fused(): pl.pallas_call(functools.partial(kernel, heads), out_shape=pltpu.VMEM((ro...  29.4 us
    unnamed x1, local copies, waits for them, and re-layouts  0.88 us

profile of v3, /device:TPU:0, one launch (start us, length us, event | category | flops | bytes accessed | tf_op | source)
XLA Modules:
  0.0 30.3 jit_solution(5448139615200638285)
XLA Ops:
  0.0 29.4 %shard_map.64 = bf16[256,1536]{1,0:T(8,128)(2,1)S(1)} custom-call(s32[4]{0:T(128)} %ids_hbm.1, s32[1,4]{1,0:T(1,128)} %tiles_hbm.1, s32[8,8,12]{2,1,0:T(8,128)} %bitcast.1, bf16[256,1536]{1,0:T(8,128)(2,1)} %q_hbm.1, bf16[256,1536]{1,0:T(8,128)(2,1)} %k_hbm.1, bf16[256,1536]{1,0:T(8,128)(2,1)} %v_hbm.1), custom_call_target="tpu_custom_call" | custom-call | tf_op jit(solution)/shard_map/pallas_call | solution.py:242
  29.4 0.9 %copy.8 = bf16[256,1536]{1,0:T(8,128)(2,1)} copy(bf16[256,1536]{1,0:T(8,128)(2,1)S(1)} %shard_map.64) | data formatting | bytes 1572864
